TPU v7x, 32 devices: a whole 2x2x4 slice. The times are simulated.
32 devices in a mesh: pipe: 2 (over core), dp: 8 (over z, y), tensor: 2 (over x).
Axes of the slice: x: 2, y: 2, z: 4, core: 2. Of those that a mesh axis runs over, the one named last changes fastest.
Arguments:
- tokens: bfloat16 [2, 8, 64, 1024], P(None, 'dp'), may hold values from -6 to 6
- conv_grid: bfloat16 [2, 8, 8, 8, 1536], P(None, 'dp'), may hold values from -6 to 6
- order: int32 [8, 2], P('dp'), may hold values from 0 to 1, as said below
- trainable: int32 [2, 5], P('pipe'), may hold values from 0 to 1, as said below
- ln_attn: bfloat16 [2, 1024], P('pipe', 'dp'), may hold values from 0.099609375 to 1.8984375
- w_qkv: bfloat16 [2, 3, 1024, 1024], P('pipe', None, 'dp', 'tensor'), may hold values from -0.1875 to 0.1875
- w_attn_out: bfloat16 [2, 1024, 1024], P('pipe', 'tensor', 'dp'), may hold values from -1.5 to 1.5
- ln_mlp: bfloat16 [2, 1024], P('pipe', 'dp'), may hold values from 0.099609375 to 1.8984375
- w_fc_in: bfloat16 [2, 1024, 4096], P('pipe', 'dp', 'tensor'), may hold values from -0.1875 to 0.1875
- w_fc_out: bfloat16 [2, 4096, 1024], P('pipe', 'tensor', 'dp'), may hold values from -0.09375 to 0.09375
- conv_depth: bfloat16 [2, 49, 1536], P('pipe', None, 'dp'), may hold values from -0.875 to 0.875
- ln_conv: bfloat16 [2, 1536], P('pipe', 'dp'), may hold values from 0.099609375 to 1.8984375
- w_pw_in: bfloat16 [2, 1536, 6144], P('pipe', 'dp', 'tensor'), may hold values from -0.15625 to 0.15625
- w_pw_out: bfloat16 [2, 6144, 1536], P('pipe', 'tensor', 'dp'), may hold values from -0.078125 to 0.078125
- layer_scale: bfloat16 [2, 1536], P('pipe', 'dp'), may hold values from 0.5 to 1.5
- w_adapt: bfloat16 [2, 1536, 1024], P('pipe', 'dp', 'tensor'), may hold values from -0.15625 to 0.15625
- adapt_depth: bfloat16 [2, 9, 1024], P('pipe', None, 'tensor'), may hold values from -2 to 2
- w_gate_in: bfloat16 [2, 1024, 512], P('pipe', 'tensor', 'dp'), may hold values from -2 to 2
- w_gate_out: bfloat16 [2, 512, 1024], P('pipe', 'dp', 'tensor'), may hold values from -0.25 to 0.25
- tok_cot: bfloat16 [2, 8, 64, 1024], P(None, 'dp'), may hold values from -6 to 6
- grid_cot: bfloat16 [2, 8, 8, 8, 1536], P(None, 'dp'), may hold values from -6 to 6
Outputs:
- hidden_tokens: bfloat16 [2, 2, 8, 64, 1024], P('pipe', None, 'dp')
- hidden_grids: bfloat16 [2, 2, 8, 8, 8, 1536], P('pipe', None, 'dp')
- token_grads: bfloat16 [2, 2, 8, 64, 1024], P('pipe', None, 'dp')
- grid_grads: bfloat16 [2, 2, 8, 8, 8, 1536], P('pipe', None, 'dp')
- grad_ln_attn: float32 [2, 1024], P('pipe', 'dp')
- grad_w_qkv: float32 [2, 3, 1024, 1024], P('pipe', None, 'dp', 'tensor')
- grad_w_attn_out: float32 [2, 1024, 1024], P('pipe', 'tensor', 'dp')
- grad_ln_mlp: float32 [2, 1024], P('pipe', 'dp')
- grad_w_fc_in: float32 [2, 1024, 4096], P('pipe', 'dp', 'tensor')
- grad_w_fc_out: float32 [2, 4096, 1024], P('pipe', 'tensor', 'dp')
- grad_conv_depth: float32 [2, 49, 1536], P('pipe', None, 'dp')
- grad_ln_conv: float32 [2, 1536], P('pipe', 'dp')
- grad_w_pw_in: float32 [2, 1536, 6144], P('pipe', 'dp', 'tensor')
- grad_w_pw_out: float32 [2, 6144, 1536], P('pipe', 'tensor', 'dp')
- grad_layer_scale: float32 [2, 1536], P('pipe', 'dp')
- grad_w_adapt: float32 [2, 1536, 1024], P('pipe', 'dp', 'tensor')
- grad_adapt_depth: float32 [2, 9, 1024], P('pipe', None, 'tensor')
- grad_w_gate_in: float32 [2, 1024, 512], P('pipe', 'tensor', 'dp')
- grad_w_gate_out: float32 [2, 512, 1024], P('pipe', 'dp', 'tensor')
Inputs may be any that keep to these rules, and one draw needn't show every extreme that they name: `order`: each row holds every micro-batch number exactly once. Each weight is trained in exactly one of the two layers: trainable[1, j] = 1 - trainable[0, j].
All inputs are finite; a program needn't handle non-finite values.
Results may differ from a plain program's by a relative error of at most 0.04.
Values may be sent and summed in bfloat16 or wider, within the bound.
A program may use at most 320 MiB of HBM per device.

v0:
```python
import functools

import jax
import jax.numpy as jnp
from jax import lax
from jax.experimental import pallas as pl
from jax.experimental.pallas import tpu as pltpu
from jax.sharding import PartitionSpec as P

HD = 64
Z = 4
R = 2
TOK = 64
SIDE = 8
LANE = 128
BF = jnp.bfloat16
F32 = jnp.float32
ARRAYS = ("P1", "P2", "Q", "O", "E", "Gi", "Go", "F1", "F2")
EVENTS = (
    "n1", "f", "o", "cv", "n2", "c2", "m", "br", "gs",
    "dx3", "dgh", "dn2", "dc2", "dx1", "dcv", "dn1", "df", "gv", "gad",
)


def mm(a, b):
    return lax.dot_general(a, b, (((1,), (0,)), ((), ())), preferred_element_type=F32)


def mm_nt(a, b):
    return lax.dot_general(a, b, (((1,), (1,)), ((), ())), preferred_element_type=F32)


def mm_tn(a, b):
    return lax.dot_general(a, b, (((0,), (0,)), ((), ())), preferred_element_type=F32)


def flat(value):
    return value.reshape(-1, value.shape[-1])


def low(value):
    return value.astype(BF)


def wide(value):
    return value.astype(F32)


def gelu_pair(h):
    phi = 0.5 * (1.0 + lax.erf(h * 0.7071067811865476))
    dens = jnp.exp(-0.5 * h * h) * 0.3989422804014327
    return h * phi, phi + h * dens


def normed(value):
    centred = value - jnp.mean(value, axis=-1, keepdims=True)
    rs = lax.rsqrt(jnp.mean(centred * centred, axis=-1, keepdims=True) + 1e-06)
    return centred * rs, rs


def norm_back(dn, n_hat, rs, gain):
    gd = dn * gain
    return (
        gd
        - jnp.mean(gd, axis=-1, keepdims=True)
        - n_hat * jnp.mean(gd * n_hat, axis=-1, keepdims=True)
    ) * rs


def col_shift(value, by):
    if by == 0:
        return value
    at = lax.broadcasted_iota(jnp.int32, value.shape, 0) % SIDE
    rolled = pltpu.roll(value, (-by) % TOK, 0)
    return jnp.where((at + by >= 0) & (at + by < SIDE), rolled, 0.0)


def row_shift(value, by):
    if by == 0:
        return value
    gap = jnp.zeros((abs(by) * SIDE, value.shape[1]), value.dtype)
    if by > 0:
        return jnp.concatenate([value[by * SIDE :], gap], axis=0)
    return jnp.concatenate([gap, value[: TOK + by * SIDE]], axis=0)


def depthwise(value, tap, side):
    half = side // 2
    shifted = [col_shift(value, b - half) for b in range(side)]
    total = None
    for a in range(side):
        line = None
        for b in range(side):
            term = shifted[b] * tap(a * side + b)
            line = term if line is None else line + term
        line = row_shift(line, a - half)
        total = line if total is None else total + line
    return total


def depthwise_taps(value, grad, side, put):
    half = side // 2
    shifted = [col_shift(value, b - half) for b in range(side)]
    for a in range(side):
        d = a - half
        lo, hi = max(0, -d) * SIDE, (SIDE - max(0, d)) * SIDE
        for b in range(side):
            part = shifted[b][lo + d * SIDE : hi + d * SIDE] * grad[lo:hi]
            put(a * side + b, jnp.sum(part, axis=0, keepdims=True))


def lanes_of(at, width):
    return pl.ds(pl.multiple_of(at * width, width), width)


def side_by_side(blocks):
    return jnp.concatenate(blocks, axis=1)


def main_kernel(dims, outer, *refs):
    at = iter(refs)

    def take(count):
        return [next(at) for _ in range(count)]

    na = len(ARRAYS)
    source = dict(zip(ARRAYS, take(na)))
    (
        depth_in, ln_conv_in, scale_in, ln_attn_in, ln_mlp_in, adapt_depth_in,
        order_in, train_in, tok_in, grid_in, tcot_in, gcot_in,
    ) = take(12)
    hid_tok, hid_grid, out_gtok, out_ggrid = take(4)
    native = dict(zip(ARRAYS, take(na)))
    out_depth, out_ln_conv, out_scale, out_ln_attn, out_ln_mlp, out_ad = take(6)
    W = dict(zip(ARRAYS, take(na)))
    hops = take(4 * na)
    RX = {name: hops[4 * n : 4 * n + 4] for n, name in enumerate(ARRAYS)}
    (
        v_loc, v_low, vv, aq, vec_c, vec_d, x_in, c_in, n1_all, f_all, n2_all, c2_all,
        o_sb, o_rb, cv_sb, cv_rb, m_sb, m_rb, br_sb, br_rb, gsb, dgb,
        qkv, prob, ctx, u, up, r, rp, cn, crs, cv_sum, x1, c2f,
        adapted, spread, pooled, gate,
        dx3, dcot, dx3_all, dn2_sb, dn2_rb, dc2_sb, dc2_rb, dx1_all, dcv_all,
        dn1_sb, dn1_rb, df_sb, df_rb, dh, do_all, dqkv, dhc, dx1, dc2t, dad, dcn,
        gvs, gvs_low, gv_rb, gvx, gad, gad_rb, gad_all, turned,
    ) = take(67)
    (
        zs_send, zs_recv, l_send, l_recv, s1_send, s1_recv, loc_sem, s2_send, s2_recv,
        v_send, v_recv, q_send, q_recv, h_send, h_recv, b_send, b_recv, c_send, c_recv,
        xo_send, xo_recv, g_send, g_recv, a_send, a_recv, gx_send, gx_recv, go,
    ) = take(28)

    p = lax.axis_index("pipe")
    dpi = lax.axis_index("dp")
    x = lax.axis_index("tensor")
    rest = dpi % outer
    zi = dpi // (outer * R)
    ri = (dpi // outer) % R
    xo = 1 - x
    ro = 1 - ri
    d_dim, c_dim, hq, ffq, cfq, adq, dg = dims
    adh = Z * adq
    dz, cz = d_dim // Z, c_dim // Z
    tile = 256
    ids = {name: number for number, name in enumerate(ARRAYS)}
    ev = {name: number for number, name in enumerate(EVENTS)}

    def dev(z=None, rr=None, xx=None, pp=None):
        z = zi if z is None else z
        rr = ri if rr is None else rr
        return (
            p if pp is None else pp,
            (z * R + rr) * outer + rest,
            x if xx is None else xx,
        )

    def zto(d):
        return lax.rem(zi + d, Z)

    def zfrom(d):
        return lax.rem(zi + Z - d, Z)

    def remote(src, dst, ssem, rsem, device):
        return pltpu.make_async_remote_copy(
            src_ref=src, dst_ref=dst, send_sem=ssem, recv_sem=rsem,
            device_id=device, device_id_type=pl.DeviceIdType.MESH,
        )

    sib = dev(pp=1 - p)
    over_r, over_x = dev(rr=ro), dev(xx=xo)

    def z_copy(e, d, src, dst):
        return remote(src, dst, zs_send.at[e, d - 1], zs_recv.at[e, d - 1], dev(zto(d)))

    sent = []

    def gather_copies(name, buf):
        return [z_copy(ev[name], d, buf.at[zi], buf.at[zi]) for d in range(1, Z)]

    def gather_start(name, buf, keep=True):
        copies = gather_copies(name, buf)
        for c in copies:
            c.start()
        if keep:
            sent.extend(copies)

    def gather_wait(name, buf):
        for d in range(1, Z):
            slot = buf.at[zfrom(d)]
            z_copy(ev[name], d, slot, slot).wait_recv()

    def scatter_start(name, sb, rb):
        for d in range(1, Z):
            c = z_copy(ev[name], d, sb.at[zto(d)], rb.at[d - 1])
            c.start()
            sent.append(c)

    def scatter_wait(name, rb):
        for d in range(1, Z):
            z_copy(ev[name], d, rb.at[d - 1], rb.at[d - 1]).wait_recv()

    def right():
        return dev(zi + 1)

    def left():
        return dev(zi - 1)

    def pass_copy(name, buf, toward, s):
        e, k = ev[name], (0 if toward > 0 else 3) + s
        blk = buf.at[zi - toward * s]
        return remote(blk, blk, l_send.at[e, k], l_recv.at[e, k], right() if toward > 0 else left())

    def pass_cond(toward, s):
        if toward > 0:
            return (zi < Z - 1) & (zi - s >= 0)
        return (zi > 0) & (zi + s <= Z - 1)

    def line_start(name, buf):
        for toward in (1, -1):

            @pl.when(pass_cond(toward, 0))
            def _():
                pass_copy(name, buf, toward, 0).start()

    def line_step(name, buf, *steps):
        e = ev[name]
        for s in steps:
            for toward in (1, -1):
                src = zi - toward * s

                @pl.when((src >= 0) & (src <= Z - 1))
                def _():
                    blk = buf.at[src]
                    k = (0 if toward > 0 else 3) + s - 1
                    remote(blk, blk, l_send.at[e, k], l_recv.at[e, k], sib).wait_recv()

                if s < Z - 1:

                    @pl.when(pass_cond(toward, s))
                    def _():
                        pass_copy(name, buf, toward, s).start()

    def line_sent(name, buf):
        for toward in (1, -1):
            for s in range(Z - 1):

                @pl.when(pass_cond(toward, s))
                def _():
                    pass_copy(name, buf, toward, s).wait_send()

    def sum_copy(name, sb, rb, toward, k, first):
        e, way = ev[name], (0 if toward > 0 else 1)
        src = sb.at[zi + toward * k] if first else rb.at[way, k]
        q = way * 3 + k - 1
        return remote(src, rb.at[way, k - 1], l_send.at[e, q], l_recv.at[e, q], right() if toward > 0 else left())

    def at_end(toward):
        return zi == (0 if toward > 0 else Z - 1)

    def passes(toward, k):
        dest = zi + toward * k
        return jnp.logical_not(at_end(toward)) & (dest >= 0) & (dest <= Z - 1)

    def sum_start(name, sb, rb):
        for toward in (1, -1):

            @pl.when(at_end(toward))
            def _():
                for k in (3, 2, 1):
                    sum_copy(name, sb, rb, toward, k, True).start()

    def sum_arrival(name, rb, way, k):
        e = ev[name]
        slot = rb.at[way, k]
        return remote(slot, slot, l_send.at[e, way * 3 + k], l_recv.at[e, way * 3 + k], sib)

    def sum_step(name, sb, rb, *ks):
        for k in ks:
            for way, toward in enumerate((1, -1)):

                @pl.when(passes(toward, k))
                def _():
                    sum_arrival(name, rb, way, k).wait_recv()
                    rb[way, k] = low(wide(rb[way, k]) + wide(sb[zi + toward * k]))
                    sum_copy(name, sb, rb, toward, k, False).start()

    def sum_wait(name, rb):
        for way, toward in enumerate((1, -1)):

            @pl.when(jnp.logical_not(at_end(toward)))
            def _():
                sum_arrival(name, rb, way, 0).wait_recv()

    def summed(sb, rb):
        return wide(sb[zi]) + (wide(rb[0, 0]) + wide(rb[1, 0]))

    def sum_sent(name, sb, rb):
        for toward in (1, -1):

            @pl.when(at_end(toward))
            def _():
                for k in (3, 2, 1):
                    sum_copy(name, sb, rb, toward, k, True).wait_send()

            for k in (2, 1):

                @pl.when(passes(toward, k))
                def _():
                    sum_copy(name, sb, rb, toward, k, False).wait_send()

    def share_start(name, buf):
        for d in range(1, Z):
            c = z_copy(ev[name], d, buf.at[3], buf.at[d - 1])
            c.start()
            sent.append(c)

    def scattered(sb, rb):
        return (wide(sb[zi]) + wide(rb[0])) + (wide(rb[1]) + wide(rb[2]))

    barrier = pltpu.get_barrier_semaphore()
    greeted = [sib]
    for d in range(1, Z):
        greeted += [dev(zto(d)), dev(zto(d), ro), dev(zto(d), pp=1 - p)]
    greeted += [over_r, over_x, dev(rr=ro, xx=xo)]
    for device in greeted:
        pl.semaphore_signal(barrier, inc=1, device_id=device, device_id_type=pl.DeviceIdType.MESH)
    v_loc[...] = jnp.zeros(v_loc.shape, F32)
    taps7 = depth_in.shape[0]
    c_own = depth_in.shape[1]
    v_loc[0:taps7, 0:c_own] = wide(depth_in[...])
    v_loc[49:50, 0:c_own] = wide(ln_conv_in[...])
    v_loc[50:51, 0:c_own] = wide(scale_in[...])
    v_loc[56:57, 0:LANE] = wide(ln_attn_in[...])
    v_loc[57:58, 0:LANE] = wide(ln_mlp_in[...])
    aq[x] = jnp.zeros(aq.shape[1:], F32)
    aq[x, 0:9] = wide(adapt_depth_in[:, lanes_of(zi, adq)])
    v_low[...] = low(v_loc[...])
    line_sums = (
        ("o", o_sb, o_rb), ("cv", cv_sb, cv_rb), ("m", m_sb, m_rb), ("dn2", dn2_sb, dn2_rb),
        ("dc2", dc2_sb, dc2_rb), ("dn1", dn1_sb, dn1_rb), ("df", df_sb, df_rb),
    )
    line_gathers = (
        ("n1", n1_all), ("f", f_all), ("n2", n2_all), ("c2", c2_all), ("dx1", dx1_all), ("dcv", dcv_all),
    )
    for _, _, rb in line_sums:
        for way, toward in enumerate((1, -1)):

            @pl.when(at_end(toward))
            def _():
                rb[way, 0] = jnp.zeros(rb.shape[2:], BF)

    pl.semaphore_wait(barrier, len(greeted))

    me8 = zi * R + ri
    v_arrivals = []
    for n, (d, flip) in enumerate([(d, s) for d in range(Z) for s in (0, 1)][1:]):
        tr = ro if flip else ri
        c = remote(v_low, vv.at[me8], v_send.at[n], v_recv.at[n], dev(zto(d), tr))
        c.start()
        sent.append(c)
        fr = zfrom(d) * R + tr
        v_arrivals.append(remote(vv.at[fr], vv.at[fr], v_send.at[n], v_recv.at[n], dev(zto(d), tr)))
    vv[me8] = v_low[...]
    c = remote(aq.at[x], aq.at[x], q_send, q_recv, over_x)
    c.start()
    sent.append(c)

    by_rows = ("O", "F2")

    def quarter_of(name, ref, z):
        if name == "Q":
            return ref.at[:, :, lanes_of(z, hq)]
        if name in by_rows:
            height = ref.shape[0] // Z
            return ref.at[pl.ds(pl.multiple_of(z * height, height), height)]
        return ref.at[:, lanes_of(z, ref.shape[1] // Z)]

    def step1_local(name):
        return pltpu.make_async_copy(
            quarter_of(name, source[name], zi), W[name].at[x, zi, ri], loc_sem.at[ids[name]]
        )

    def step1_copy(name, d):
        k = ids[name]
        return remote(
            quarter_of(name, source[name], zto(d)), W[name].at[x, zi, ri],
            s1_send.at[k, d - 1], s1_recv.at[k, d - 1], dev(zto(d)),
        )

    def half_of(name, j, z, rr, upper):
        w = W[name]
        half = w.shape[-2] // 2
        rows = slice(half, None) if upper else slice(0, half)
        if len(w.shape) == 6:
            return w.at[j, z, rr, :, rows]
        return w.at[j, z, rr, rows]

    def step2_copy(name, which, d):
        k = ids[name]
        z = zfrom(d)
        if which < 2:
            src = quarter_of(name, source[name], zi) if d == 0 else W[name].at[x, z, ri]
            dst = W[name].at[x, z, ri]
        else:
            src = dst = half_of(name, x, z, ro, False) if which == 2 else half_of(name, xo, z, ri, True)
        to = over_x if which in (1, 2) else over_r
        return remote(src, dst, s2_send.at[k, which, d], s2_recv.at[k, which, d], to)

    def step2_arrival(name, which, d):
        k = ids[name]
        z = zfrom(d)
        if which < 2:
            ref = W[name].at[x, z, ro] if which == 0 else W[name].at[xo, z, ri]
        else:
            ref = half_of(name, xo, z, ro, which == 3)
        to = over_x if which in (1, 2) else over_r
        return remote(ref, ref, s2_send.at[k, which, d], s2_recv.at[k, which, d], to)

    def relay1(*names):
        for name in names:
            for d in range(1, Z):
                step1_copy(name, d).start()

    def relay0(*names):
        for name in names:
            step1_local(name).start()
            step2_copy(name, 0, 0).start()
            step2_copy(name, 1, 0).start()

    def relay2(name, ds=(1, 2, 3)):
        k = ids[name]
        for d in ds:
            slot = W[name].at[x, zfrom(d), ri]
            remote(slot, slot, s1_send.at[k, d - 1], s1_recv.at[k, d - 1], dev(zto(d))).wait_recv()
            step2_copy(name, 0, d).start()
            step2_copy(name, 1, d).start()

    def relay3(name, ds=(0, 1, 2, 3)):
        for d in ds:
            step2_arrival(name, 0, d).wait_recv()
            step2_copy(name, 2, d).start()
            step2_arrival(name, 1, d).wait_recv()
            step2_copy(name, 3, d).start()

    def relay4(*names):
        for name in names:
            step1_local(name).wait()
            for d in range(Z):
                step2_arrival(name, 2, d).wait_recv()
                step2_arrival(name, 3, d).wait_recv()

    def relay_sent():
        for name in ARRAYS:
            for d in range(1, Z):
                step1_copy(name, d).wait_send()
            for which in range(4):
                for d in range(Z):
                    step2_copy(name, which, d).wait_send()

    @pl.when(p == 0)
    def _():
        relay0("P1")
        relay1("P1")
        relay0("P2")
        relay1("P2")
        relay0("Q", "O", "E", "Gi", "Go", "F1", "F2")

    @pl.when(p == 1)
    def _():
        dx3[...] = tcot_in[x]
        dcot[...] = gcot_in[x]
        dx3_all[zi] = tcot_in[x]
        line_start("dx3", dx3_all)

    for c in v_arrivals:
        c.wait_recv()
    remote(aq.at[xo], aq.at[xo], q_send, q_recv, over_x).wait_recv()
    low_lanes = lax.broadcasted_iota(jnp.int32, (64, LANE), 1) < LANE // 2
    for z in range(Z):
        first, second = wide(vv[2 * z]), pltpu.roll(wide(vv[2 * z + 1]), LANE // 2, 1)
        vec_c[:, z * cz : z * cz + LANE] = first[:, 0:LANE]
        vec_c[:, z * cz + LANE : z * cz + 2 * LANE] = jnp.where(
            low_lanes, first[:, LANE:], second[:, 0:LANE]
        )
        vec_c[:, z * cz + 2 * LANE : (z + 1) * cz] = second[:, LANE:]
    for i in range(Z * R):
        vec_d[:, i * LANE : (i + 1) * LANE] = wide(vv[i])[56:64, 0:LANE]

    def gain_d(row):
        return vec_d[row : row + 1, :]

    def gain_c(row):
        return vec_c[row : row + 1, :]

    def token_entry():
        n_hat, _ = normed(wide(x_in[...]))
        n1_all[zi] = low(n_hat * gain_d(0))
        line_start("n1", n1_all)

    def conv_entry():
        @pl.loop(0, c_dim // LANE)
        def _(ch):
            lanes = lanes_of(ch, LANE)
            taps = vec_c[:, lanes]
            cn[:, lanes] = depthwise(wide(c_in[:, lanes]), lambda k: taps[k : k + 1], 7)

        n_hat, rs = normed(cn[...])
        cn[...] = n_hat
        crs[...] = jnp.broadcast_to(rs, crs.shape)
        f_all[zi] = low(n_hat * gain_c(49))
        line_start("f", f_all)

    def first_relays(pump):
        relay2("P1")
        pump(1)
        relay1("Q", "O")
        relay2("P2")
        pump(2)
        relay3("P1")


    @pl.when(p == 0)
    def _():
        first = order_in[0, x] == 0
        c_in[...] = jnp.where(first, grid_in[0], grid_in[1])
        x_in[...] = jnp.where(first, tok_in[0], tok_in[1])
        conv_entry()
        token_entry()

        def pump(s):
            line_step("f", f_all, s)
            line_step("n1", n1_all, s)

        first_relays(pump)
        line_step("f", f_all, 3)
        line_step("n1", n1_all, 3)

    @pl.when(p == 1)
    def _():
        pl.semaphore_wait(go, 1)
        relay0("P1")
        relay1("P1")
        relay0("P2")
        relay1("P2")
        relay0("Q", "O", "E", "Gi", "Go", "F1", "F2")
        first_relays(lambda s: line_step("dx3", dx3_all, s))
        remote(c_in, c_in, h_send.at[1], h_recv.at[1], sib).wait_recv()
        conv_entry()
        line_step("dx3", dx3_all, 3)
        line_step("f", f_all, 1)

    relay2("Q")
    relay2("O")
    relay1("E", "Gi", "Go")
    relay3("P2", (0, 1))

    @pl.when(p == 1)
    def _():
        line_step("f", f_all, 2, 3)

    relay4("P1")

    def conv_hidden(j):
        act, der = gelu_pair(mm(flat(f_all[...]), flat(W["P1"][j])))
        r[j] = low(act)
        rp[j] = low(der)

    conv_hidden(0)

    relay3("P2", (2, 3))
    for name in ("E", "Gi", "Go"):
        relay2(name)
    relay1("F1")
    conv_hidden(1)
    relay3("Q")
    relay3("O")
    relay2("F1")
    relay1("F2")

    @pl.when(p == 0)
    def _():
        pl.semaphore_signal(go, inc=1, device_id=sib, device_id_type=pl.DeviceIdType.MESH)

    relay4("P2")

    def pair_rows(name, pair):
        zs = pl.ds(pair * 2, 2)
        return side_by_side([flat(W[name][0, zs]), flat(W[name][1, zs])])

    def pair_out(left, name, sb, width):
        both = side_by_side([left[0], left[1]])

        @pl.loop(0, Z // 2)
        def _(pair):
            acc = mm_nt(both, pair_rows(name, pair))
            sb[:, :, lanes_of(pair, 2 * width)] = low(acc).reshape(Z, TOK, 2 * width)

    pair_out(r, "P2", cv_sb, cz)

    sum_start("cv", cv_sb, cv_rb)

    for name in ("E", "Gi", "Go"):
        relay3(name)
    sum_step("cv", cv_sb, cv_rb, 2)
    relay2("F2")
    sum_step("cv", cv_sb, cv_rb, 1)

    @pl.when(p == 1)
    def _():
        remote(x_in, x_in, h_send.at[0], h_recv.at[0], sib).wait_recv()
        token_entry()
        line_step("n1", n1_all, 1, 2, 3)

    relay4("Q", "O")
    wide_q = side_by_side([flat(W["Q"][j, :, :, s]) for j in range(2) for s in range(3)])
    qkv_both = low(mm(flat(n1_all[...]), wide_q))
    for j in range(2):
        qkv[j] = qkv_both[:, j * 3 * hq : (j + 1) * 3 * hq]
    @pl.loop(0, Z)
    def _(b):
        rows = lanes_of(b, TOK)
        for j in range(2):
            outs = []
            for h in range(hq // HD):
                q, kk, vals = (qkv[j, rows, s * hq + h * HD : s * hq + (h + 1) * HD] for s in range(3))
                sc = mm_nt(q, kk) * HD ** (-0.5)
                e = jnp.exp(sc - jnp.max(sc, axis=-1, keepdims=True))
                pr = low(e / jnp.sum(e, axis=-1, keepdims=True))
                prob[j, h, b] = pr
                outs.append(mm(pr, vals))
            ctx[j, rows, :] = low(side_by_side(outs))

    out_cols = [
        jnp.concatenate([W["O"][0, z, rr], W["O"][1, z, rr]], axis=0) for z in range(Z) for rr in range(R)
    ]
    o_sb[...] = low(mm(side_by_side([ctx[0], ctx[1]]), side_by_side(out_cols))).reshape(Z, TOK, d_dim)
    sum_start("o", o_sb, o_rb)

    relay3("F1")

    sum_wait("cv", cv_rb)
    cv_sum[...] = summed(cv_sb, cv_rb)
    c2f[...] = wide(c_in[...]) + gain_c(50) * cv_sum[...]
    c2_low = low(c2f[...])
    c2_all[zi] = c2_low
    line_start("c2", c2_all)
    sum_step("o", o_sb, o_rb, 2)
    hid_grid[x] = c2_low

    @pl.when(p == 0)
    def _():
        remote(hid_grid.at[x], c_in, h_send.at[1], h_recv.at[1], sib).start()

    relay3("F2")
    sum_step("o", o_sb, o_rb, 1)
    line_step("c2", c2_all, 1)
    sum_wait("o", o_rb)
    x1[...] = wide(x_in[...]) + summed(o_sb, o_rb)
    n_hat, _ = normed(x1[...])
    n2_all[zi] = low(n_hat * gain_d(1))
    line_start("n2", n2_all)

    relay4("E", "Gi", "Go")
    line_step("c2", c2_all, 2)
    line_step("n2", n2_all, 1)
    line_step("c2", c2_all, 3)
    row8 = lax.broadcasted_iota(jnp.int32, (8, adq), 0)
    gs_part = None
    ad_both = mm(flat(c2_all[...]), side_by_side([flat(W["E"][0]), flat(W["E"][1])]))
    for j in range(2):
        ad = ad_both[:, j * adq : (j + 1) * adq]
        adapted[j] = ad
        taps = aq[j]
        pool = jnp.zeros((8, adq), F32)
        for b in range(Z):
            sp = depthwise(ad[b * TOK : (b + 1) * TOK], lambda k: taps[k : k + 1], 3)
            spread[j, b] = sp
            pool = jnp.where(row8 == b, jnp.mean(sp, axis=0, keepdims=True), pool)
        pooled[j] = pool
        term = mm_nt(low(pool), flat(W["Gi"][j]))
        gs_part = term if gs_part is None else gs_part + term
    gsb[3] = gs_part
    share_start("gs", gsb)
    line_step("n2", n2_all, 2)

    relay4("F1")
    line_step("n2", n2_all, 3)
    for j in range(2):
        act, der = gelu_pair(mm(flat(n2_all[...]), flat(W["F1"][j])))
        u[j] = low(act)
        up[j] = low(der)

    scatter_wait("gs", gsb)

    def gate_hidden():
        return gelu_pair((gsb[0] + gsb[1]) + (gsb[2] + gsb[3]))

    gh, _ = gate_hidden()
    for j in range(2):
        g8 = jnp.tanh(mm(low(gh), flat(W["Go"][j])))
        gate[j] = g8
        for b in range(Z):
            br_sb[b, :, j * adq : (j + 1) * adq] = low(g8[b : b + 1] * spread[j, b])
    scatter_start("br", br_sb, br_rb)
    relay4("F2")

    u_both = side_by_side([u[0], u[1]])

    @pl.loop(0, Z // 2)
    def _(pair):
        halves = [
            side_by_side([W["F2"][j, 2 * pair + dz_, rr] for dz_ in range(2) for rr in range(R)])
            for j in range(2)
        ]
        acc = mm(u_both, jnp.concatenate(halves, axis=0))
        m_sb[:, :, lanes_of(pair, 2 * dz)] = low(acc).reshape(Z, TOK, 2 * dz)

    sum_start("m", m_sb, m_rb)

    def exchange(n, buf):
        remote(buf.at[x], buf.at[x], xo_send.at[n], xo_recv.at[n], over_x).start()

    def layer_output(total):
        sum_step("m", m_sb, m_rb, 2)
        scatter_wait("br", br_rb)
        total[...] = x1[...]
        for d in range(Z):
            piece = br_sb[zi] if d == 0 else br_rb[d - 1]
            for j in range(2):
                lanes = pl.ds(pl.multiple_of(j * adh + zfrom(d) * adq, LANE), adq)
                total[:, lanes] += wide(piece[:, j * adq : (j + 1) * adq])
        sum_step("m", m_sb, m_rb, 1)
        sum_wait("m", m_rb)
        hid_tok[x] = low(total[...] + summed(m_sb, m_rb))

    @pl.when(p == 0)
    def _():
        layer_output(dx1)
        remote(hid_tok.at[x], x_in, h_send.at[0], h_recv.at[0], sib).start()
        exchange(0, hid_tok)

    exchange(1, hid_grid)
    relay_sent()

    def over_cores(d):
        return remote(
            out_gtok.at[x], dx3_all.at[zi], b_send.at[d], b_recv.at[d], dev(zto(d), pp=1 - p)
        )

    @pl.when(p == 0)
    def _():
        for d in range(Z):
            slot = dx3_all.at[zfrom(d)]
            remote(slot, slot, b_send.at[d], b_recv.at[d], sib).wait_recv()
        dx3[...] = dx3_all[zi]

    def own_lanes(j):
        return pl.ds(pl.multiple_of(j * adh + zi * adq, LANE), adq)

    gh, ghp = gate_hidden()
    dgh_part = None
    dgp = []
    for j in range(2):
        dgate = jnp.zeros((8, adq), F32)
        for b in range(Z):
            dbr = wide(dx3_all[b, :, own_lanes(j)])
            dgate = jnp.where(row8 == b, jnp.sum(dbr * spread[j, b], axis=0, keepdims=True), dgate)
        dg8 = low(dgate * (1.0 - gate[j] * gate[j]))
        dgp.append(dg8)
        term = mm_nt(dg8, flat(W["Go"][j]))
        dgh_part = term if dgh_part is None else dgh_part + term
    dgb[3] = dgh_part
    share_start("dgh", dgb)

    for j in range(2):
        cols = side_by_side([W["F2"][j, z, rr] for z in range(Z) for rr in range(R)])
        dh[j] = low(mm_nt(flat(dx3_all[...]), cols) * wide(up[j]))

    scatter_wait("dgh", dgb)
    dgs = low(((dgb[0] + dgb[1]) + (dgb[2] + dgb[3])) * ghp)
    for j in range(2):
        dpool = mm(dgs, flat(W["Gi"][j])) * (1.0 / TOK)
        taps = aq[j]
        tap_rows = [None] * 9
        for b in range(Z):
            dsp = gate[j, b : b + 1] * wide(dx3_all[b, :, own_lanes(j)]) + dpool[b : b + 1]
            dad[j, b * TOK : (b + 1) * TOK] = low(depthwise(dsp, lambda k: taps[8 - k : 9 - k], 3))

            def put(k, row):
                tap_rows[k] = row if tap_rows[k] is None else tap_rows[k] + row

            depthwise_taps(adapted[j, b * TOK : (b + 1) * TOK], dsp, 3, put)
        for k in range(9):
            gad[j, k : k + 1] = tap_rows[k]
        gad[j, 9:16] = jnp.zeros((7, adq), F32)

    pair_out(dad, "E", dc2_sb, cz)

    sum_start("dc2", dc2_sb, dc2_rb)

    pair_out(dh, "F1", dn2_sb, dz)

    sum_start("dn2", dn2_sb, dn2_rb)
    sum_step("dc2", dc2_sb, dc2_rb, 2)

    def half_rows(name, upper):
        half = W[name].shape[-2] // 2
        rows = slice(half, None) if upper else slice(0, half)
        return (slice(None), rows) if len(W[name].shape) == 6 else (rows,)

    fine = ("P1", "P2")

    def pieces(name):
        return (1, 2, 3, 0) if name in fine else (None,)

    def block_at(d):
        return slice(None) if d is None else zto(d)

    def hop_copy(name, which, d):
        n = ids[name]
        lower, upper = half_rows(name, False), half_rows(name, True)
        z = block_at(d)
        w, buf = W[name], RX[name]
        src, dst, to = (
            lambda: (w.at[(xo, z, slice(None)) + lower], buf[0].at[z], over_x),
            lambda: (w.at[(slice(None), z, ro) + upper], buf[1].at[:, z], over_r),
            lambda: (buf[0].at[z, ro], buf[2].at[z], over_r),
            lambda: (buf[1].at[xo, z], buf[3].at[z], over_x),
        )[which]()
        k = 0 if d is None else d
        return remote(src, dst, g_send.at[n, which, k], g_recv.at[n, which, k], to)

    def reduce_start(name, d=None):
        hop_copy(name, 0, d).start()
        hop_copy(name, 1, d).start()

    def each_block(d, body):
        if d is None:
            pl.loop(0, Z)(body)
        else:
            body(zto(d))

    def per_piece(name, body):
        if name in fine:
            pl.loop(0, Z)(lambda k: body(lax.rem(k + 1, Z)))
        else:
            body(None)

    def reduce_middle(*names):
        for name in names:
            lower, upper = half_rows(name, False), half_rows(name, True)
            buf = RX[name]

            def middle(d):
                hop_copy(name, 0, d).wait_recv()

                def add_lower(z):
                    for rr in range(R):
                        own = W[name][(x, z, rr) + lower]
                        buf[0][z, rr] = low(wide(own) + wide(buf[0][z, rr]))

                each_block(d, add_lower)
                hop_copy(name, 2, d).start()
                hop_copy(name, 1, d).wait_recv()

                def add_upper(z):
                    for j in range(2):
                        own = W[name][(j, z, ri) + upper]
                        buf[1][j, z] = low(wide(own) + wide(buf[1][j, z]))

                each_block(d, add_upper)
                hop_copy(name, 3, d).start()

            per_piece(name, middle)

    def reduce_end(*names):
        for name in names:
            lower, upper = half_rows(name, False), half_rows(name, True)
            buf = RX[name]

            def end(d):
                hop_copy(name, 2, d).wait_recv()
                hop_copy(name, 3, d).wait_recv()

                def add_both(z):
                    W[name][(x, z, ri) + lower] = low(wide(buf[0][z, ri]) + wide(buf[2][z]))
                    W[name][(x, z, ri) + upper] = low(wide(buf[1][x, z]) + wide(buf[3][z]))

                each_block(d, add_both)

            if name in fine:

                @pl.loop(1, Z)
                def _(d):
                    end(d)
                    back_copy(name, d).start()

                end(0)
            else:
                end(None)
                for d in range(1, Z):
                    back_copy(name, d).start()
            back_local(name).start()

    def back_copy(name, d):
        n = ids[name]
        return remote(
            W[name].at[x, zto(d), ri], quarter_of(name, native[name], zi),
            a_send.at[n, d - 1], a_recv.at[n, d - 1], dev(zto(d)),
        )

    def back_local(name):
        return pltpu.make_async_copy(
            W[name].at[x, zi, ri], quarter_of(name, native[name], zi), loc_sem.at[ids[name]]
        )

    peers = ((1, 0), (0, 1), (1, 1))

    def owner(k):
        return (ro if peers[k][0] else ri), (xo if peers[k][1] else x)

    def row_grad(name, left, right):
        width = W[name].shape[3]
        span = R * width

        @pl.loop(0, Z)
        def _(k):
            d = lax.rem(k + 1, Z)
            z = zto(d)
            turned[0:span] = flat(left[:, :, lanes_of(z, span)]).T
            for j in range(2):
                W[name][j, z] = low(mm(turned[0:span], right[j])).reshape(R, width, -1)
            if name in fine:
                reduce_start(name, d)

        if name not in fine:
            reduce_start(name)

    def col_grad(name, left, right):
        width = left.shape[2]
        for j in range(2):
            turned[j * width : (j + 1) * width] = left[j].T

        @pl.loop(0, Z)
        def _(z):
            rhs = flat(right[:, :, lanes_of(z, dz)])
            for j in range(2):
                g = low(mm(turned[j * width : (j + 1) * width], rhs))
                for rr in range(R):
                    W[name][j, z, rr] = g[:, rr * LANE : (rr + 1) * LANE]

        reduce_start(name)

    for j in range(2):
        W["Gi"][j] = low(mm_tn(dgs, low(pooled[j]))).reshape(Z, R, -1, adq)
        W["Go"][j] = low(mm_tn(low(gh), dgp[j])).reshape(Z, R, -1, adq)
    sum_step("dc2", dc2_sb, dc2_rb, 1)
    sum_step("dn2", dn2_sb, dn2_rb, 2)
    reduce_start("Gi")
    reduce_start("Go")
    row_grad("E", c2_all, dad)
    sum_step("dn2", dn2_sb, dn2_rb, 1)

    @pl.when(p == 0)
    def _():
        remote(dcot, dcot, c_send, c_recv, sib).wait_recv()

    sum_wait("dc2", dc2_rb)
    dc2t[...] = wide(dcot[...]) + summed(dc2_sb, dc2_rb)
    gvs_ls = jnp.sum(cv_sum[...] * dc2t[...], axis=0, keepdims=True)
    dcv_all[zi] = low(dc2t[...] * gain_c(50))
    line_start("dcv", dcv_all)

    sum_wait("dn2", dn2_rb)
    dn2 = summed(dn2_sb, dn2_rb)
    n_hat, rs = normed(x1[...])
    gvs_d1 = jnp.sum(dn2 * n_hat, axis=0, keepdims=True)
    dx1[...] = wide(dx3[...]) + norm_back(dn2, n_hat, rs, gain_d(1))
    dx1_all[zi] = low(dx1[...])
    line_start("dx1", dx1_all)
    line_step("dcv", dcv_all, 1)
    col_grad("F2", u, dx3_all)
    line_step("dcv", dcv_all, 2)
    line_step("dx1", dx1_all, 1)
    row_grad("F1", n2_all, dh)

    line_step("dcv", dcv_all, 3)
    line_step("dx1", dx1_all, 2)
    for j in range(2):
        dhc[j] = low(mm(flat(dcv_all[...]), flat(W["P2"][j])) * wide(rp[j]))

    pair_out(dhc, "P1", df_sb, cz)

    sum_start("df", df_sb, df_rb)

    early = ("Gi", "Go", "E", "F2", "F1")

    def pw_grads():
        row_grad("P2", dcv_all, r)
        row_grad("P1", f_all, dhc)

    line_step("dx1", dx1_all, 3)

    @pl.when(p == 0)
    def _():
        pw_grads()

    sum_step("df", df_sb, df_rb, 2)

    out_rows = [
        side_by_side([W["O"][j, z, rr] for z in range(Z) for rr in range(R)]) for j in range(2)
    ]
    do_both = low(mm_nt(flat(dx1_all[...]), jnp.concatenate(out_rows, axis=0)))
    for j in range(2):
        do_all[j] = do_both[:, j * hq : (j + 1) * hq]
    @pl.loop(0, Z)
    def _(b):
        rows = lanes_of(b, TOK)
        for j in range(2):
            parts = [[], [], []]
            for h in range(hq // HD):
                q, kk, vals = (qkv[j, rows, s * hq + h * HD : s * hq + (h + 1) * HD] for s in range(3))
                do = do_all[j, rows, h * HD : (h + 1) * HD]
                pr = prob[j, h, b]
                dp = mm_nt(do, vals)
                prw = wide(pr)
                ds = low(prw * (dp - jnp.sum(dp * prw, axis=-1, keepdims=True)) * HD ** (-0.5))
                parts[0].append(mm(ds, kk))
                parts[1].append(mm_tn(ds, q))
                parts[2].append(mm_tn(pr, do))
            for s in range(3):
                dqkv[j, rows, s * hq : (s + 1) * hq] = low(side_by_side(parts[s]))

    dqkv_both = side_by_side([dqkv[0], dqkv[1]])

    @pl.loop(0, Z // 2)
    def _(pair):
        zs = pl.ds(pair * 2, 2)
        rows_q = side_by_side([flat(W["Q"][j, zs, :, s]) for j in range(2) for s in range(3)])
        acc = mm_nt(dqkv_both, rows_q)
        dn1_sb[:, :, lanes_of(pair, 2 * dz)] = low(acc).reshape(Z, TOK, 2 * dz)

    sum_start("dn1", dn1_sb, dn1_rb)
    sum_step("df", df_sb, df_rb, 1)
    reduce_middle("Gi", "Go", "E")

    def attention_grads():
        @pl.loop(0, Z)
        def _(z):
            turned[0:dz] = flat(n1_all[:, :, lanes_of(z, dz)]).T
            for j in range(2):
                g = low(mm(turned[0:dz], dqkv[j]))
                for s in range(3):
                    W["Q"][j, z, :, s] = g[:, s * hq : (s + 1) * hq].reshape(R, -1, hq)

        reduce_start("Q")
        col_grad("O", ctx, dx1_all)

    sum_step("dn1", dn1_sb, dn1_rb, 2)
    reduce_middle("F2", "F1")
    sum_step("dn1", dn1_sb, dn1_rb, 1)

    @pl.when(p == 0)
    def _():
        reduce_middle("P2")
        attention_grads()
        reduce_middle("P1")
        reduce_end(*early)

    sum_wait("dn1", dn1_rb)
    dn1 = summed(dn1_sb, dn1_rb)
    n_hat, rs = normed(wide(x_in[...]))
    gvs_d0 = jnp.sum(dn1 * n_hat, axis=0, keepdims=True)
    out_gtok[x] = low(dx1[...] + norm_back(dn1, n_hat, rs, gain_d(0)))

    @pl.when(p == 1)
    def _():
        for d in (1, 2, 3, 0):
            over_cores(d).start()

    sum_wait("df", df_rb)
    dfv = summed(df_sb, df_rb)
    gvs_lc = jnp.sum(dfv * cn[...], axis=0, keepdims=True)
    dcn[...] = norm_back(dfv, cn[...], crs[:, 0:1], gain_c(49))

    @pl.loop(0, c_dim // LANE)
    def _(ch):
        lanes = lanes_of(ch, LANE)
        taps = vec_c[:, lanes]
        back = depthwise(dcn[:, lanes], lambda k: taps[48 - k : 49 - k], 7)
        out_ggrid[x, :, lanes] = low(dc2t[:, lanes] + back)

    @pl.when(p == 1)
    def _():
        remote(out_ggrid.at[x], dcot, c_send, c_recv, sib).start()
        pw_grads()
        attention_grads()
        layer_output(dx1)
        exchange(0, hid_tok)
        reduce_end(*early)

    @pl.when(p == 0)
    def _():
        reduce_end("P2")

    exchange(2, out_gtok)
    exchange(3, out_ggrid)

    @pl.loop(0, Z)
    def _(z):
        for part in range(cz // LANE):
            lanes = pl.ds(pl.multiple_of(z * cz + part * LANE, LANE), LANE)

            def put(k, row):
                gvs[z, k : k + 1, part * LANE : (part + 1) * LANE] = row

            depthwise_taps(wide(c_in[:, lanes]), dcn[:, lanes], 7, put)

    for z in range(Z):
        gvs[z, 49:50] = gvs_lc[:, z * cz : (z + 1) * cz]
        gvs[z, 50:51] = gvs_ls[:, z * cz : (z + 1) * cz]
        gvs[z, 51:64] = jnp.zeros((13, cz), F32)
        gvs[z, 56:57, 0:dz] = gvs_d0[:, z * dz : (z + 1) * dz]
        gvs[z, 57:58, 0:dz] = gvs_d1[:, z * dz : (z + 1) * dz]
    gvs_low[...] = low(gvs[...])
    scatter_start("gv", gvs_low, gv_rb)

    def group_copy(n, k, src, dst):
        rr, xx = owner(k)
        return remote(src, dst, gx_send.at[n, k], gx_recv.at[n, k], dev(rr=rr, xx=xx))

    for k in range(3):
        c = group_copy(1, k, gad, gad_rb.at[k])
        c.start()
        sent.append(c)
    @pl.when(p == 1)
    def _():
        reduce_middle("P2", "P1")
        reduce_end("P2")

    reduce_end("P1")
    scatter_wait("gv", gv_rb)
    gvx[3] = (gvs[zi] + wide(gv_rb[0])) + (wide(gv_rb[1]) + wide(gv_rb[2]))
    for k in range(3):
        c = group_copy(0, k, gvx.at[3], gvx.at[k])
        c.start()
        sent.append(c)
    for k in range(3):
        group_copy(1, k, gad, gad_rb.at[k]).wait_recv()
    gad_all[zi] = (gad[x] + gad_rb[0, x]) + (gad_rb[1, x] + gad_rb[2, x])
    gather_start("gad", gad_all)

    reduce_middle("Q", "O")
    reduce_end("Q", "O")

    for k in range(3):
        group_copy(0, k, gvx.at[k], gvx.at[k]).wait_recv()
    total = (gvx[0] + gvx[1]) + (gvx[2] + gvx[3])
    mine = jnp.where(ri == 1, pltpu.roll(total, c_own, 1), total)[:, 0:c_own]
    mine_d = jnp.where(ri == 1, total[:, LANE : 2 * LANE], total[:, 0:LANE])

    def flag(n):
        return train_in[0, n].astype(F32)

    out_depth[...] = mine[0:taps7] * flag(0)
    out_ln_conv[...] = mine[49:50] * flag(1)
    out_scale[...] = mine[50:51] * flag(4)
    out_ln_attn[...] = mine_d[56:57]
    out_ln_mlp[...] = mine_d[57:58]
    gather_wait("gad", gad_all)
    for z in range(Z):
        out_ad[:, z * adq : (z + 1) * adq] = gad_all[z][0:9]
    for name in ARRAYS:
        back_local(name).wait()
        for d in range(1, Z):
            n = ids[name]
            slot = quarter_of(name, native[name], zfrom(d))
            remote(slot, slot, a_send.at[n, d - 1], a_recv.at[n, d - 1], dev(zto(d))).wait_recv()
    for n, buf in enumerate((hid_tok, hid_grid, out_gtok, out_ggrid)):
        c = remote(buf.at[x], buf.at[x], xo_send.at[n], xo_recv.at[n], over_x)
        c.wait_send()
        remote(buf.at[xo], buf.at[xo], xo_send.at[n], xo_recv.at[n], over_x).wait_recv()

    @pl.when(p == 0)
    def _():
        remote(hid_tok.at[x], x_in, h_send.at[0], h_recv.at[0], sib).wait_send()
        remote(hid_grid.at[x], c_in, h_send.at[1], h_recv.at[1], sib).wait_send()

    @pl.when(p == 1)
    def _():
        for d in range(Z):
            over_cores(d).wait_send()
        remote(out_ggrid.at[x], dcot, c_send, c_recv, sib).wait_send()

    for name, buf in line_gathers:
        line_sent(name, buf)

    @pl.when(p == 1)
    def _():
        line_sent("dx3", dx3_all)

    for name, sb, rb in line_sums:
        sum_sent(name, sb, rb)
    for c in sent:
        c.wait_send()
    for name in ARRAYS:
        for which in range(4):
            for d in pieces(name):
                hop_copy(name, which, d).wait_send()
        for d in range(1, Z):
            back_copy(name, d).wait_send()


def run_layers(weights, vectors, order, train, streams, sizes, outer):
    d_dim, c_dim, hq, ffq, cfq, adw, dg = sizes
    vm = pltpu.VMEM
    blocks = []
    for name, value in zip(ARRAYS, weights):
        if name == "Q":
            blocks.append((3, value.shape[1], hq))
        elif name in ("O", "F2"):
            blocks.append((value.shape[0] // Z, value.shape[1]))
        else:
            blocks.append((value.shape[0], value.shape[1] // Z))
    rows = Z * TOK

    def act(width, count=Z, kind=BF):
        return vm((count, TOK, width), kind)

    def line(width):
        return vm((2, 3, TOK, width), BF)

    scratch = [vm((2, Z, R) + s, BF) for s in blocks] + [
        vm(lead + s[:-2] + (s[-2] // 2, s[-1]), BF)
        for s in blocks
        for lead in ((Z, R), (2, Z), (Z,), (Z,))
    ]
    scratch += [
        vm((64, 2 * LANE), F32), vm((64, 2 * LANE), BF), vm((Z * R, 64, 2 * LANE), BF), vm((2, 16, adw), F32), vm((64, c_dim), F32), vm((8, d_dim), F32),
        vm((TOK, d_dim), BF), vm((TOK, c_dim), BF), act(d_dim), act(c_dim), act(d_dim), act(c_dim),
        act(d_dim), line(d_dim), act(c_dim), line(c_dim), act(d_dim), line(d_dim),
        act(2 * adw), act(2 * adw, 3), vm((4, 8, dg), F32), vm((4, 8, dg), F32),
        vm((2, rows, 3 * hq), BF), vm((2, hq // HD, Z, TOK, TOK), BF), vm((2, rows, hq), BF),
        vm((2, rows, ffq), BF), vm((2, rows, ffq), BF), vm((2, rows, cfq), BF), vm((2, rows, cfq), BF),
        vm((TOK, c_dim), F32), vm((TOK, LANE), F32), vm((TOK, c_dim), F32), vm((TOK, d_dim), F32), vm((TOK, c_dim), F32),
        vm((2, rows, adw), F32), vm((2, Z, TOK, adw), F32), vm((2, 8, adw), F32), vm((2, 8, adw), F32),
        vm((TOK, d_dim), BF), vm((TOK, c_dim), BF), act(d_dim), act(d_dim), line(d_dim), act(c_dim), line(c_dim),
        act(d_dim), act(c_dim),
        act(d_dim), line(d_dim), act(c_dim), line(c_dim), vm((2, rows, ffq), BF), vm((2, rows, hq), BF),
        vm((2, rows, 3 * hq), BF), vm((2, rows, cfq), BF), vm((TOK, d_dim), F32), vm((TOK, c_dim), F32), vm((2, rows, adw), BF),
        vm((TOK, c_dim), F32),
        vm((Z, 64, c_dim // Z), F32), vm((Z, 64, c_dim // Z), BF), vm((3, 64, c_dim // Z), BF), vm((4, 64, c_dim // Z), F32),
        vm((2, 16, adw), F32), vm((3, 2, 16, adw), F32), vm((Z, 16, adw), F32),
        vm((2 * ffq, rows), BF),
    ]
    dma = pltpu.SemaphoreType.DMA
    na = len(ARRAYS)
    scratch += [
        dma((len(EVENTS), 3)), dma((len(EVENTS), 3)), dma((len(EVENTS), 6)), dma((len(EVENTS), 6)), dma((na, 3)), dma((na, 3)), dma((na,)),
        dma((na, 4, Z)), dma((na, 4, Z)), dma((7,)), dma((7,)), dma, dma, dma((2,)), dma((2,)), dma((Z,)), dma((Z,)), dma, dma,
        dma((4,)), dma((4,)), dma((na, 4, Z)), dma((na, 4, Z)), dma((na, 3)), dma((na, 3)), dma((2, 3)), dma((2, 3)),
        pltpu.SemaphoreType.REGULAR,
    ]
    sds = jax.ShapeDtypeStruct
    out_shape = [sds((2, TOK, d_dim), BF), sds((2, TOK, c_dim), BF)] * 2
    out_shape += [sds(value.shape, BF) for value in weights]
    out_shape += [sds(value.shape, F32) for value in vectors]
    any_spec = pl.BlockSpec(memory_space=pl.ANY)
    vm_spec = pl.BlockSpec(memory_space=pltpu.VMEM)
    sm_spec = pl.BlockSpec(memory_space=pltpu.SMEM)
    return pl.pallas_call(
        functools.partial(main_kernel, sizes, outer),
        out_shape=out_shape,
        in_specs=[any_spec] * na + [vm_spec] * 6 + [sm_spec] * 2 + [vm_spec] * 4,
        out_specs=[vm_spec] * 4 + [any_spec] * na + [vm_spec] * 6,
        scratch_shapes=scratch,
        compiler_params=pltpu.CompilerParams(
            collective_id=0, has_side_effects=True, vmem_limit_bytes=62 * 1024 * 1024
        ),
        cost_estimate=pl.CostEstimate(flops=26 * 10**9, bytes_accessed=10**8, transcendentals=10**7),
        name="layers",
    )(*weights, *vectors, order, train, *streams)


def finish_kernel(flagged, layer_zero, count, *refs):
    grads, streams, vectors = refs[:count], refs[count : count + 4], refs[count + 4 : count + 10]
    order, train = refs[count + 10 : count + 12]
    refs = refs[count + 12 :]
    out_grads, out_streams, out_vectors = refs[:count], refs[count : count + 4], refs[count + 4 : count + 10]
    refs = refs[count + 10 :]
    held, wide_ones = refs[:count], refs[count : 2 * count]
    in_sem, out_sem = refs[2 * count :]

    def fetch(n):
        return pltpu.make_async_copy(grads[n], held[n], in_sem.at[n])

    def put_back(n):
        return pltpu.make_async_copy(wide_ones[n], out_grads[n], out_sem.at[n])

    for n in range(count):
        fetch(n).start()
    swap = (lax.axis_index("pipe") == layer_zero) & (order[0, 0] == 1)
    for n, (src, dst) in enumerate(zip(streams, out_streams)):
        for m in range(2):
            dst[m] = src[m] if n < 2 else jnp.where(swap, src[1 - m], src[m])
    for src, dst in zip(vectors, out_vectors):
        dst[...] = src[...]
    for n in range(count):
        fetch(n).wait()
        src, dst = held[n], wide_ones[n]
        scale = train[0, flagged[n]].astype(F32) if n in flagged else None
        lead = src.shape[0] if len(src.shape) == 3 else 1

        @pl.loop(0, lead * (src.shape[-2] // 16))
        def _(step):
            rows = pl.ds(pl.multiple_of((step // lead) * 16, 16), 16)
            at = (step % lead, rows) if len(src.shape) == 3 else (rows,)
            value = wide(src[at])
            dst[at] = value if scale is None else value * scale

        put_back(n).start()
    for n in range(count):
        put_back(n).wait()


def finish(outs, order, train):
    count = len(ARRAYS)
    streams, grads, vectors = outs[:4], outs[4 : 4 + count], outs[4 + count :]
    any_spec = pl.BlockSpec(memory_space=pl.ANY)
    sm_spec = pl.BlockSpec(memory_space=pltpu.SMEM)
    vm_spec = pl.BlockSpec(memory_space=pltpu.VMEM)
    sds = jax.ShapeDtypeStruct
    dma = pltpu.SemaphoreType.DMA
    flagged = {ARRAYS.index("P1"): 2, ARRAYS.index("P2"): 3}
    return pl.pallas_call(
        functools.partial(finish_kernel, flagged, 0, count),
        out_shape=[sds(g.shape, F32) for g in grads]
        + [sds(value.shape, value.dtype) for value in (*streams, *vectors)],
        in_specs=[any_spec] * count + [vm_spec] * 10 + [sm_spec] * 2,
        out_specs=[any_spec] * count + [vm_spec] * 10,
        scratch_shapes=[pltpu.VMEM(g.shape, BF) for g in grads]
        + [pltpu.VMEM(g.shape, F32) for g in grads]
        + [dma((count,)), dma((count,))],
        compiler_params=pltpu.CompilerParams(vmem_limit_bytes=62 * 1024 * 1024),
        name="finish",
    )(*grads, *streams, *vectors, order, train)


def per_device(
    tokens,
    conv_grid,
    order,
    trainable,
    ln_attn,
    w_qkv,
    w_attn_out,
    ln_mlp,
    w_fc_in,
    w_fc_out,
    conv_depth,
    ln_conv,
    w_pw_in,
    w_pw_out,
    layer_scale,
    w_adapt,
    adapt_depth,
    w_gate_in,
    w_gate_out,
    tok_cot,
    grid_cot,
):
    dp_count = lax.axis_size("dp")
    outer = dp_count // (Z * R)
    groups = [[g * outer + o for o in range(outer)] for g in range(Z * R)]

    def block(value, axis):
        value = value[0]
        if outer == 1:
            return value
        return lax.all_gather(value, "dp", axis=axis, tiled=True, axis_index_groups=groups)

    def share(value, axis):
        if outer > 1:
            value = lax.psum_scatter(
                value, "dp", scatter_dimension=axis, tiled=True, axis_index_groups=groups
            )
        return value[None]

    qkv = block(w_qkv, 1)
    gate_in = block(w_gate_in, 1).T
    pw_in = block(w_pw_in, 0)
    adapt = block(w_adapt, 0)
    fc_in = block(w_fc_in, 0)
    weights = (
        pw_in,
        block(w_pw_out, 1).T,
        qkv,
        block(w_attn_out, 1),
        adapt,
        gate_in,
        block(w_gate_out, 0),
        fc_in,
        block(w_fc_out, 1),
    )
    vectors = (
        block(conv_depth, 1),
        block(ln_conv, 0)[None],
        block(layer_scale, 0)[None],
        block(ln_attn, 0)[None],
        block(ln_mlp, 0)[None],
        adapt_depth[0],
    )
    spread = Z * R
    sizes = (
        qkv.shape[1] * spread, pw_in.shape[0] * spread, qkv.shape[2] // Z, fc_in.shape[1] // Z,
        pw_in.shape[1] // Z, adapt.shape[1] // Z, gate_in.shape[0] * spread,
    )

    def rows_of(value):
        return value.reshape(value.shape[0], TOK, value.shape[-1])

    streams = [rows_of(value) for value in (tokens, conv_grid, tok_cot, grid_cot)]
    outs = run_layers(weights, vectors, order, trainable, streams, sizes, outer)
    done = finish(outs, order, trainable)
    g_p1, g_p2, g_q, g_o, g_e, g_gi, g_go, g_f1, g_f2 = done[:9]
    hid_tok, hid_grid, g_tok, g_grid = done[9:13]
    g_depth, g_ln_conv, g_scale, g_ln_attn, g_ln_mlp, g_ad = done[13:]
    grid_shape = (1,) + conv_grid.shape
    tok_shape = (1,) + tokens.shape
    if outer > 1:
        g_ad = lax.psum(g_ad, "dp", axis_index_groups=groups)
    return (
        hid_tok.reshape(tok_shape),
        hid_grid.reshape(grid_shape),
        g_tok.reshape(tok_shape),
        g_grid.reshape(grid_shape),
        share(g_ln_attn[0], 0),
        share(g_q, 1),
        share(g_o, 1),
        share(g_ln_mlp[0], 0),
        share(g_f1, 0),
        share(g_f2, 1),
        share(g_depth, 1),
        share(g_ln_conv[0], 0),
        share(g_p1, 0),
        share(g_p2.T, 1),
        share(g_scale[0], 0),
        share(g_e, 0),
        g_ad[None],
        share(g_gi.T, 1),
        share(g_go, 0),
    )


def solution(mesh):
    in_specs = (
        P(None, "dp", None, None),
        P(None, "dp", None, None, None),
        P("dp", None),
        P("pipe", None),
        P("pipe", "dp"),
        P("pipe", None, "dp", "tensor"),
        P("pipe", "tensor", "dp"),
        P("pipe", "dp"),
        P("pipe", "dp", "tensor"),
        P("pipe", "tensor", "dp"),
        P("pipe", None, "dp"),
        P("pipe", "dp"),
        P("pipe", "dp", "tensor"),
        P("pipe", "tensor", "dp"),
        P("pipe", "dp"),
        P("pipe", "dp", "tensor"),
        P("pipe", None, "tensor"),
        P("pipe", "tensor", "dp"),
        P("pipe", "dp", "tensor"),
        P(None, "dp", None, None),
        P(None, "dp", None, None, None),
    )
    out_specs = (
        P("pipe", None, "dp", None, None),
        P("pipe", None, "dp", None, None, None),
        P("pipe", None, "dp", None, None),
        P("pipe", None, "dp", None, None, None),
        P("pipe", "dp"),
        P("pipe", None, "dp", "tensor"),
        P("pipe", "tensor", "dp"),
        P("pipe", "dp"),
        P("pipe", "dp", "tensor"),
        P("pipe", "tensor", "dp"),
        P("pipe", None, "dp"),
        P("pipe", "dp"),
        P("pipe", "dp", "tensor"),
        P("pipe", "tensor", "dp"),
        P("pipe", "dp"),
        P("pipe", "dp", "tensor"),
        P("pipe", None, "tensor"),
        P("pipe", "tensor", "dp"),
        P("pipe", "dp", "tensor"),
    )
    return jax.shard_map(
        per_device, mesh=mesh, in_specs=in_specs, out_specs=out_specs, check_vma=False
    )
```

profile of v0, /device:TPU:0, one launch (start us, length us, event | category | flops | bytes accessed | tf_op | source)
XLA Modules:
  0.0 436.0 jit_solution(345536233930513814)
XLA Ops:
  0.7 425.0 %layers.1 = (bf16[2,64,1024]{2,1,0:T(8,128)(2,1)}, bf16[2,64,1536]{2,1,0:T(8,128)(2,1)}, bf16[2,64,1024]{2,1,0:T(8,128)(2,1)}, bf16[2,64,1536]{2,1,0:T(8,128)(2,...) custom-call(bf16[192,3072]{1,0:T(8,128)(2,1)} %bitcast.50, ...), custom_call_target="tpu_custom_call" | custom-call | flops 25999998976 | bytes 100000000 | tf_op jit(solution)/shard_map/layers/pallas_call | solution.py:1291
  425.7 7.4 %finish.1 = (f32[192,3072]{1,0:T(8,128)}, f32[192,3072]{1,0:T(8,128)}, f32[3,128,512]{2,1,0:T(8,128)}, f32[512,128]{1,0:T(8,128)}, f32[192,512]{1,0:T(8,128)}, /...) custom-call(bf16[192,3072]{1,0:T(8,128)(2,1)} %get-tuple-element.57., ...), custom_call_target="tpu_custom_call" | custom-call | tf_op jit(solution)/shard_map/finish/pallas_call | solution.py:1355
  433.1 1.4 copy.45
  434.5 1.5 copy.44
where the time goes:
time: 436 us
  Pallas kernels  432 us (99%)
    pallas_call x1, Pallas kernels, run_layers(): pl.pallas_call(functools.partial(main_kernel, sizes, outer), out_shape=ou...  425 us

commit v1 on v0

--- a/solution.py
+++ b/solution.py
@@ -133,8 +133,8 @@
     native = dict(zip(ARRAYS, take(na)))
     out_depth, out_ln_conv, out_scale, out_ln_attn, out_ln_mlp, out_ad = take(6)
     W = dict(zip(ARRAYS, take(na)))
-    hops = take(4 * na)
-    RX = {name: hops[4 * n : 4 * n + 4] for n, name in enumerate(ARRAYS)}
+    hops = take(4 * (na - 1))
+    RX = {name: hops[4 * max(n - 1, 0) : 4 * max(n - 1, 0) + 4] for n, name in enumerate(ARRAYS)}
     (
         v_loc, v_low, vv, aq, vec_c, vec_d, x_in, c_in, n1_all, f_all, n2_all, c2_all,
         o_sb, o_rb, cv_sb, cv_rb, m_sb, m_rb, br_sb, br_rb, gsb, dgb,
@@ -142,13 +142,14 @@
         adapted, spread, pooled, gate,
         dx3, dcot, dx3_all, dn2_sb, dn2_rb, dc2_sb, dc2_rb, dx1_all, dcv_all,
         dn1_sb, dn1_rb, df_sb, df_rb, dh, do_all, dqkv, dhc, dx1, dc2t, dad, dcn,
-        gvs, gvs_low, gv_rb, gvx, gad, gad_rb, gad_all, turned,
-    ) = take(67)
+        gvs, gvs_low, gv_rb, gvx, gad, gad_rb, gad_all, turned, alt_a, alt_b, nat,
+    ) = take(70)
     (
         zs_send, zs_recv, l_send, l_recv, s1_send, s1_recv, loc_sem, s2_send, s2_recv,
         v_send, v_recv, q_send, q_recv, h_send, h_recv, b_send, b_recv, c_send, c_recv,
         xo_send, xo_recv, g_send, g_recv, a_send, a_recv, gx_send, gx_recv, go,
-    ) = take(28)
+        m_send, m_recv, f_sem, f_send, f_recv,
+    ) = take(33)
 
     p = lax.axis_index("pipe")
     dpi = lax.axis_index("dp")
@@ -922,16 +923,19 @@
                     back_copy(name, d).start()
             back_local(name).start()
 
+    def landing(name):
+        return nat if name in ("P1", "P2") else native[name]
+
     def back_copy(name, d):
         n = ids[name]
         return remote(
-            W[name].at[x, zto(d), ri], quarter_of(name, native[name], zi),
+            W[name].at[x, zto(d), ri], quarter_of(name, landing(name), zi),
             a_send.at[n, d - 1], a_recv.at[n, d - 1], dev(zto(d)),
         )
 
     def back_local(name):
         return pltpu.make_async_copy(
-            W[name].at[x, zi, ri], quarter_of(name, native[name], zi), loc_sem.at[ids[name]]
+            W[name].at[x, zi, ri], quarter_of(name, landing(name), zi), loc_sem.at[ids[name]]
         )
 
     peers = ((1, 0), (0, 1), (1, 1))
@@ -1006,6 +1010,31 @@
 
     line_step("dcv", dcv_all, 3)
     line_step("dx1", dx1_all, 2)
+
+    def operand_copies():
+        return [
+            remote(src, dst, m_send.at[n], m_recv.at[n], sib)
+            for n, (src, dst) in enumerate(((dcv_all, alt_a), (r, alt_b)))
+        ]
+
+    def operand_copies_back():
+        return [
+            remote(src, dst, m_send.at[n], m_recv.at[n], sib)
+            for n, (src, dst) in enumerate(((f_all, alt_a), (dhc, alt_b)))
+        ]
+
+    def chosen(flag_at, left, right):
+        for n, buf in enumerate((alt_a, alt_b)):
+            remote(buf, buf, m_send.at[n], m_recv.at[n], sib).wait_recv()
+        mine = train_in[0, flag_at] == 1
+        alt_a[...] = jnp.where(mine, left[...], alt_a[...])
+        alt_b[...] = jnp.where(mine, right[...], alt_b[...])
+
+    @pl.when(p == 1)
+    def _():
+        for c in operand_copies():
+            c.start()
+
     for j in range(2):
         dhc[j] = low(mm(flat(dcv_all[...]), flat(W["P2"][j])) * wide(rp[j]))
 
@@ -1016,8 +1045,10 @@
     early = ("Gi", "Go", "E", "F2", "F1")
 
     def pw_grads():
-        row_grad("P2", dcv_all, r)
-        row_grad("P1", f_all, dhc)
+        for c in operand_copies_back():
+            c.start()
+        chosen(3, dcv_all, r)
+        row_grad("P2", alt_a, alt_b)
 
     line_step("dx1", dx1_all, 3)
 
@@ -1084,7 +1115,6 @@
     def _():
         reduce_middle("P2")
         attention_grads()
-        reduce_middle("P1")
         reduce_end(*early)
 
     sum_wait("dn1", dn1_rb)
@@ -1113,7 +1143,6 @@
     @pl.when(p == 1)
     def _():
         remote(out_ggrid.at[x], dcot, c_send, c_recv, sib).start()
-        pw_grads()
         attention_grads()
         layer_output(dx1)
         exchange(0, hid_tok)
@@ -1153,12 +1182,6 @@
         c = group_copy(1, k, gad, gad_rb.at[k])
         c.start()
         sent.append(c)
-    @pl.when(p == 1)
-    def _():
-        reduce_middle("P2", "P1")
-        reduce_end("P2")
-
-    reduce_end("P1")
     scatter_wait("gv", gv_rb)
     gvx[3] = (gvs[zi] + wide(gv_rb[0])) + (wide(gv_rb[1]) + wide(gv_rb[2]))
     for k in range(3):
@@ -1169,9 +1192,37 @@
         group_copy(1, k, gad, gad_rb.at[k]).wait_recv()
     gad_all[zi] = (gad[x] + gad_rb[0, x]) + (gad_rb[1, x] + gad_rb[2, x])
     gather_start("gad", gad_all)
-
     reduce_middle("Q", "O")
     reduce_end("Q", "O")
+
+    @pl.when(p == 1)
+    def _():
+        chosen(2, f_all, dhc)
+        row_grad("P1", alt_a, alt_b)
+        reduce_middle("P1")
+        reduce_end("P1")
+
+    def to_both(name):
+        n = ids[name]
+        back_local(name).wait()
+        for d in range(1, Z):
+            slot = quarter_of(name, nat, zfrom(d))
+            remote(slot, slot, a_send.at[n, d - 1], a_recv.at[n, d - 1], dev(zto(d))).wait_recv()
+        pltpu.make_async_copy(nat, native[name], f_sem).start()
+        remote(nat, native[name], f_send, f_recv, sib).start()
+
+    def both_done(name, other):
+        pltpu.make_async_copy(nat, native[name], f_sem).wait()
+        remote(nat, native[name], f_send, f_recv, sib).wait_send()
+        remote(nat, native[other], f_send, f_recv, sib).wait_recv()
+
+    @pl.when(p == 0)
+    def _():
+        to_both("P2")
+
+    @pl.when(p == 1)
+    def _():
+        to_both("P1")
 
     for k in range(3):
         group_copy(0, k, gvx.at[k], gvx.at[k]).wait_recv()
@@ -1190,7 +1241,7 @@
     gather_wait("gad", gad_all)
     for z in range(Z):
         out_ad[:, z * adq : (z + 1) * adq] = gad_all[z][0:9]
-    for name in ARRAYS:
+    for name in ARRAYS[2:]:
         back_local(name).wait()
         for d in range(1, Z):
             n = ids[name]
@@ -1223,12 +1274,29 @@
         sum_sent(name, sb, rb)
     for c in sent:
         c.wait_send()
-    for name in ARRAYS:
+    def all_sent(name):
         for which in range(4):
             for d in pieces(name):
                 hop_copy(name, which, d).wait_send()
         for d in range(1, Z):
             back_copy(name, d).wait_send()
+
+    for name in ARRAYS[2:]:
+        all_sent(name)
+
+    @pl.when(p == 0)
+    def _():
+        all_sent("P2")
+        for c in operand_copies_back():
+            c.wait_send()
+        both_done("P2", "P1")
+
+    @pl.when(p == 1)
+    def _():
+        all_sent("P1")
+        for c in operand_copies():
+            c.wait_send()
+        both_done("P1", "P2")
 
 
 def run_layers(weights, vectors, order, train, streams, sizes, outer):
@@ -1252,7 +1320,7 @@
 
     scratch = [vm((2, Z, R) + s, BF) for s in blocks] + [
         vm(lead + s[:-2] + (s[-2] // 2, s[-1]), BF)
-        for s in blocks
+        for s in blocks[1:]
         for lead in ((Z, R), (2, Z), (Z,), (Z,))
     ]
     scratch += [
@@ -1271,7 +1339,7 @@
         vm((TOK, c_dim), F32),
         vm((Z, 64, c_dim // Z), F32), vm((Z, 64, c_dim // Z), BF), vm((3, 64, c_dim // Z), BF), vm((4, 64, c_dim // Z), F32),
         vm((2, 16, adw), F32), vm((3, 2, 16, adw), F32), vm((Z, 16, adw), F32),
-        vm((2 * ffq, rows), BF),
+        vm((2 * ffq, rows), BF), act(c_dim), vm((2, rows, cfq), BF), vm(weights[0].shape, BF),
     ]
     dma = pltpu.SemaphoreType.DMA
     na = len(ARRAYS)
@@ -1280,6 +1348,7 @@
         dma((na, 4, Z)), dma((na, 4, Z)), dma((7,)), dma((7,)), dma, dma, dma((2,)), dma((2,)), dma((Z,)), dma((Z,)), dma, dma,
         dma((4,)), dma((4,)), dma((na, 4, Z)), dma((na, 4, Z)), dma((na, 3)), dma((na, 3)), dma((2, 3)), dma((2, 3)),
         pltpu.SemaphoreType.REGULAR,
+        dma((2,)), dma((2,)), dma, dma, dma,
     ]
     sds = jax.ShapeDtypeStruct
     out_shape = [sds((2, TOK, d_dim), BF), sds((2, TOK, c_dim), BF)] * 2
@@ -1324,7 +1393,11 @@
         for m in range(2):
             dst[m] = src[m] if n < 2 else jnp.where(swap, src[1 - m], src[m])
     for src, dst in zip(vectors, out_vectors):
-        dst[...] = src[...]
+        if len(dst.shape) == 3:
+            for row in range(dst.shape[0]):
+                dst[row] = src[row : row + 1]
+        else:
+            dst[...] = src[...]
     for n in range(count):
         fetch(n).wait()
         src, dst = held[n], wide_ones[n]
@@ -1355,7 +1428,8 @@
     return pl.pallas_call(
         functools.partial(finish_kernel, flagged, 0, count),
         out_shape=[sds(g.shape, F32) for g in grads]
-        + [sds(value.shape, value.dtype) for value in (*streams, *vectors)],
+        + [sds(value.shape, value.dtype) for value in streams]
+        + [sds(value.shape if value.shape[0] == 1 else (value.shape[0], 1, value.shape[1]), F32) for value in vectors],
         in_specs=[any_spec] * count + [vm_spec] * 10 + [sm_spec] * 2,
         out_specs=[any_spec] * count + [vm_spec] * 10,
         scratch_shapes=[pltpu.VMEM(g.shape, BF) for g in grads]
@@ -1447,6 +1521,7 @@
     g_depth, g_ln_conv, g_scale, g_ln_attn, g_ln_mlp, g_ad = done[13:]
     grid_shape = (1,) + conv_grid.shape
     tok_shape = (1,) + tokens.shape
+    g_depth, g_ad = g_depth[:, 0], g_ad[:, 0]
     if outer > 1:
         g_ad = lax.psum(g_ad, "dp", axis_index_groups=groups)
     return (

time: 436 us -> 427 us (0.979)
  Pallas kernels: 432 us -> 426 us
    pallas_call x1, Pallas kernels: 425 us -> 419 us  [run_layers(): pl.pallas_call(functools.partial(main_kernel, sizes, outer), out_shape=ou...]
where the time goes in v1:
time: 427 us
  Pallas kernels  426 us (100%)
    pallas_call x1, Pallas kernels, run_layers(): pl.pallas_call(functools.partial(main_kernel, sizes, outer), out_shape=ou...  419 us

profile of v1, /device:TPU:0, one launch (start us, length us, event | category | flops | bytes accessed | tf_op | source)
XLA Modules:
  0.0 427.2 jit_solution(2102798124766986324)
XLA Ops:
  0.7 418.9 %layers.1 = (bf16[2,64,1024]{2,1,0:T(8,128)(2,1)}, bf16[2,64,1536]{2,1,0:T(8,128)(2,1)}, bf16[2,64,1024]{2,1,0:T(8,128)(2,1)}, bf16[2,64,1536]{2,1,0:T(8,128)(2,...) custom-call(bf16[192,3072]{1,0:T(8,128)(2,1)} %bitcast.48, ...), custom_call_target="tpu_custom_call" | custom-call | flops 25999998976 | bytes 100000000 | tf_op jit(solution)/shard_map/layers/pallas_call | solution.py:1360
  419.6 7.4 %finish.1 = (f32[192,3072]{1,0:T(8,128)}, f32[192,3072]{1,0:T(8,128)}, f32[3,128,512]{2,1,0:T(8,128)}, f32[512,128]{1,0:T(8,128)}, f32[192,512]{1,0:T(8,128)}, /...) custom-call(bf16[192,3072]{1,0:T(8,128)(2,1)} %get-tuple-element.57., ...), custom_call_target="tpu_custom_call" | custom-call | tf_op jit(solution)/shard_map/finish/pallas_call | solution.py:1428

commit v2 on v1

--- a/solution.py
+++ b/solution.py
@@ -1014,13 +1014,13 @@
     def operand_copies():
         return [
             remote(src, dst, m_send.at[n], m_recv.at[n], sib)
-            for n, (src, dst) in enumerate(((dcv_all, alt_a), (r, alt_b)))
+            for n, (src, dst) in enumerate(((f_all, alt_a), (dhc, alt_b)))
         ]
 
     def operand_copies_back():
         return [
             remote(src, dst, m_send.at[n], m_recv.at[n], sib)
-            for n, (src, dst) in enumerate(((f_all, alt_a), (dhc, alt_b)))
+            for n, (src, dst) in enumerate(((dcv_all, alt_a), (r, alt_b)))
         ]
 
     def chosen(flag_at, left, right):
@@ -1030,14 +1030,19 @@
         alt_a[...] = jnp.where(mine, left[...], alt_a[...])
         alt_b[...] = jnp.where(mine, right[...], alt_b[...])
 
+    @pl.when(p == 0)
+    def _():
+        for c in operand_copies_back():
+            c.start()
+
+    for j in range(2):
+        dhc[j] = low(mm(flat(dcv_all[...]), flat(W["P2"][j])) * wide(rp[j]))
+
     @pl.when(p == 1)
     def _():
         for c in operand_copies():
             c.start()
 
-    for j in range(2):
-        dhc[j] = low(mm(flat(dcv_all[...]), flat(W["P2"][j])) * wide(rp[j]))
-
     pair_out(dhc, "P1", df_sb, cz)
 
     sum_start("df", df_sb, df_rb)
@@ -1045,10 +1050,8 @@
     early = ("Gi", "Go", "E", "F2", "F1")
 
     def pw_grads():
-        for c in operand_copies_back():
-            c.start()
-        chosen(3, dcv_all, r)
-        row_grad("P2", alt_a, alt_b)
+        chosen(2, f_all, dhc)
+        row_grad("P1", alt_a, alt_b)
 
     line_step("dx1", dx1_all, 3)
 
@@ -1113,7 +1116,7 @@
 
     @pl.when(p == 0)
     def _():
-        reduce_middle("P2")
+        reduce_middle("P1")
         attention_grads()
         reduce_end(*early)
 
@@ -1150,7 +1153,7 @@
 
     @pl.when(p == 0)
     def _():
-        reduce_end("P2")
+        reduce_end("P1")
 
     exchange(2, out_gtok)
     exchange(3, out_ggrid)
@@ -1197,10 +1200,10 @@
 
     @pl.when(p == 1)
     def _():
-        chosen(2, f_all, dhc)
-        row_grad("P1", alt_a, alt_b)
-        reduce_middle("P1")
-        reduce_end("P1")
+        chosen(3, dcv_all, r)
+        row_grad("P2", alt_a, alt_b)
+        reduce_middle("P2")
+        reduce_end("P2")
 
     def to_both(name):
         n = ids[name]
@@ -1218,11 +1221,11 @@
 
     @pl.when(p == 0)
     def _():
+        to_both("P1")
+
+    @pl.when(p == 1)
+    def _():
         to_both("P2")
-
-    @pl.when(p == 1)
-    def _():
-        to_both("P1")
 
     for k in range(3):
         group_copy(0, k, gvx.at[k], gvx.at[k]).wait_recv()
@@ -1286,17 +1289,17 @@
 
     @pl.when(p == 0)
     def _():
-        all_sent("P2")
+        all_sent("P1")
         for c in operand_copies_back():
             c.wait_send()
-        both_done("P2", "P1")
+        both_done("P1", "P2")
 
     @pl.when(p == 1)
     def _():
-        all_sent("P1")
+        all_sent("P2")
         for c in operand_copies():
             c.wait_send()
-        both_done("P1", "P2")
+        both_done("P2", "P1")
 
 
 def run_layers(weights, vectors, order, train, streams, sizes, outer):

time: 427 us -> 427 us (level)
  no operation moved by 1% of the time
where the time goes in v2:
time: 427 us
  Pallas kernels  426 us (100%)
    pallas_call x1, Pallas kernels, run_layers(): pl.pallas_call(functools.partial(main_kernel, sizes, outer), out_shape=ou...  419 us

profile of v2, /device:TPU:0, one launch (start us, length us, event | category | flops | bytes accessed | tf_op | source)
XLA Modules:
  0.0 427.3 jit_solution(16868122418040046406)
XLA Ops:
  0.7 419.0 %layers.1 = (bf16[2,64,1024]{2,1,0:T(8,128)(2,1)}, bf16[2,64,1536]{2,1,0:T(8,128)(2,1)}, bf16[2,64,1024]{2,1,0:T(8,128)(2,1)}, bf16[2,64,1536]{2,1,0:T(8,128)(2,...) custom-call(bf16[192,3072]{1,0:T(8,128)(2,1)} %bitcast.48, ...), custom_call_target="tpu_custom_call" | custom-call | flops 25999998976 | bytes 100000000 | tf_op jit(solution)/shard_map/layers/pallas_call | solution.py:1363
  419.7 7.4 %finish.1 = (f32[192,3072]{1,0:T(8,128)}, f32[192,3072]{1,0:T(8,128)}, f32[3,128,512]{2,1,0:T(8,128)}, f32[512,128]{1,0:T(8,128)}, f32[192,512]{1,0:T(8,128)}, /...) custom-call(bf16[192,3072]{1,0:T(8,128)(2,1)} %get-tuple-element.57., ...), custom_call_target="tpu_custom_call" | custom-call | tf_op jit(solution)/shard_map/finish/pallas_call | solution.py:1431
